TPU v7x, 32 devices: a whole 2x2x4 slice. The times are simulated.
32 devices in a mesh: node: 4 (over z), drow: 4 (over x, core), dcol: 2 (over y).
Axes of the slice: x: 2, y: 2, z: 4, core: 2. Of those that a mesh axis runs over, the one named last changes fastest.
Arguments:
- freq_resp: bfloat16 [2, 8, 4096, 4096], P(None, None, ('drow', 'dcol'), 'node'), may hold values from -0.09375 to 0.09375
- node_coords: int32 [2, 4096], P(None, 'node'), may hold values from 0 to 1023
- heading_steps: int32 [2, 512], replicated, may hold values from -8 to 8
- spectral_weights: int32 [8, 512], replicated, may hold values from 1 to 64
Outputs:
- cross_spectra: float32 [2, 8, 4, 1024, 4096], P(None, None, 'drow', 'node', 'dcol')
All inputs are finite; a program needn't handle non-finite values.
Results may differ from a plain program's by a relative error of at most 0.0038.
Values may be sent and summed in bfloat16 or wider, within the bound.
A program may use at most 192 MiB of HBM per device.

v0:
```python
import math

import jax
import jax.numpy as jnp
from jax import lax
from jax.sharding import PartitionSpec as P

DIRS = 512
FREQS = 8
GRID = 1024


def excitation(coords, heading_steps, spectral_weights):
    freq_index = (jnp.arange(FREQS, dtype=jnp.int32) + 1)[:, None, None]
    project = (
        coords[0][:, None] * heading_steps[0][None, :]
        + coords[1][:, None] * heading_steps[1][None, :]
    )
    turn_count = jnp.mod(freq_index * project[None], GRID)
    phase_angle = turn_count.astype(jnp.float32) * (2.0 * math.pi / GRID)
    spread = jnp.sqrt(spectral_weights.astype(jnp.float32) / (64.0 * DIRS))[:, None, :]
    load_re = (spread * jnp.cos(phase_angle)).astype(jnp.bfloat16)
    load_im = (-spread * jnp.sin(phase_angle)).astype(jnp.bfloat16)
    return (load_re, load_im)


def local(freq_resp, node_coords, heading_steps, spectral_weights):
    load_re, load_im = excitation(node_coords, heading_steps, spectral_weights)
    right_re = jnp.concatenate([load_re, load_im], axis=1)
    right_im = jnp.concatenate([load_im, load_re], axis=1)
    left_re = jnp.concatenate([freq_resp[0], -freq_resp[1]], axis=2)
    left_im = jnp.concatenate([freq_resp[0], freq_resp[1]], axis=2)
    amp_re = jnp.einsum("fkn,fnd->kfd", left_re, right_re, preferred_element_type=jnp.float32)
    amp_im = jnp.einsum("fkn,fnd->kfd", left_im, right_im, preferred_element_type=jnp.float32)
    partial_amp = jnp.stack([amp_re, amp_im], axis=1)
    by_dirs = lax.psum_scatter(partial_amp, "node", scatter_dimension=3, tiled=True).astype(
        jnp.bfloat16
    )
    amplitudes = lax.all_to_all(by_dirs, "node", split_axis=0, concat_axis=3, tiled=True)
    colset = lax.all_gather(amplitudes[None], ("node", "drow"), axis=0, tiled=True)
    col_cat = jnp.concatenate([colset[:, :, 0], colset[:, :, 1]], axis=-1)
    row_piece = lax.all_gather(amplitudes, "dcol", axis=0, tiled=True)
    lead_re = jnp.concatenate([row_piece[:, 0], row_piece[:, 1]], axis=-1)
    lead_im = jnp.concatenate([row_piece[:, 1], -row_piece[:, 0]], axis=-1)
    spec_re = jnp.einsum("kfe,gsfe->fkgs", lead_re, col_cat, preferred_element_type=jnp.float32)
    spec_im = jnp.einsum("kfe,gsfe->fkgs", lead_im, col_cat, preferred_element_type=jnp.float32)
    col_width = spec_re.shape[2] * spec_re.shape[3]
    spec_re = spec_re.reshape(spec_re.shape[0], spec_re.shape[1], col_width)
    spec_im = spec_im.reshape(spec_im.shape[0], spec_im.shape[1], col_width)
    return jnp.stack([spec_re, spec_im], axis=0)[:, :, None]


def solution(mesh):
    placed = (P(None, None, ("drow", "dcol"), "node"), P(None, "node"), P(), P())
    return jax.shard_map(
        local,
        mesh=mesh,
        in_specs=placed,
        out_specs=P(None, None, "drow", "node", "dcol"),
        check_vma=False,
    )
```

profile of v0, /device:TPU:0, one launch (start us, length us, event | category | flops | bytes accessed | tf_op | source)
XLA Modules:
  0.0 828.9 jit_solution(17439720640973939558)
XLA Ops:
  6.5 0.0 reduce-scatter.2.cloned.1.call-start
  6.5 0.0 copy-start.1
  6.5 11.8 %slice_bitcast_fusion.2 = (bf16[8,512,1024]{2,1,0:T(8,128)(2,1)}, bf16[8,512,1024]{2,1,0:T(8,128)(2,1)}) fusion(bf16[2,8,512,1024]{3,2,1,0:T(8,128)(2,1)} %param.4), kind=kLoop, calls=%fused_computation.27 | loop fusion | bytes 33554432 | tf_op jit(solution)/shard_map/squeeze | solution.py:31
  18.3 0.0 copy-start.2
  18.3 0.0 copy-start
  18.3 7.2 fusion.31
  25.5 0.0 copy-done.1
  25.5 0.0 copy-done.2
  25.5 0.0 copy-done
  25.6 0.4 multiply_add_fusion
  25.9 0.0 slice-start
  25.9 71.1 %multiply_convert_fusion = (bf16[8,1024,512]{1,2,0:T(8,128)(2,1)}, bf16[8,1024,512]{1,2,0:T(8,128)(2,1)}) fusion(f32[8,512]{1,0:T(8,128)S(1)} %get-tuple-element.13, s32[1024,512]{0,1:T(8,128)S(1)} %multiply_add_fusion, s32[8]{0:T(128)S(1)} %iota_add_fusion, f32[8,512]{1,0:T(8,128)S(1)} %get-tuple-element.14), kind=kLoop, calls=%fused_computation.25 | loop fusion | flops 75497472 | bytes 18907168 | tf_op jit(solution)/shard_map/convert_element_type | solution.py:23
  97.0 0.0 slice-start.1
  97.0 17.3 %fusion.19 = f32[512,1,8,512]{0,3,2,1:T(8,128)} fusion(bf16[8,512,1024]{2,1,0:T(8,128)(2,1)} %get-tuple-element.8, bf16[8,512,1024]{2,1,0:T(8,128)(2,1)} %get-tuple-element.7, bf16[8,1024,512]{1,2,0:T(8,128)(2,1)} %get-tuple-element.12, bf16[8,1024,512]{1,2,0:T(8,128)(2,1)} %get-tuple-element.11), kind=kOutput, calls=%fused_computation.37 | convolution fusion | flops 8657043456 | bytes 41943040 | tf_op jit(solution)/shard_map/fkn,fnd->kfd/dot_general | solution.py:34
  114.3 0.0 slice-done
  114.3 0.0 slice-done.1
  114.3 16.2 %fusion.22 = f32[512,1,8,512]{0,3,2,1:T(8,128)} fusion(bf16[8,512,1024]{2,1,0:T(8,128)(2,1)} %get-tuple-element.8, bf16[8,512,1024]{2,1,0:T(8,128)(2,1)S(1)} %bitcast.60, bf16[8,1024,512]{1,2,0:T(8,128)(2,1)} %get-tuple-element.11, bf16[8,1024,512]{1,2,0:T(8,128)(2,1)} %get-tuple-element.12), kind=kOutput, calls=%fused_computation.38 | convolution fusion | flops 8657043456 | bytes 41943040 | tf_op jit(solution)/shard_map/fkn,fnd->kfd/dot_general | solution.py:33
  130.4 11.8 %pad_maximum_fusion.5 = f32[512,2,8,512]{0,3,2,1:T(8,128)} fusion(f32[512,1,8,512]{0,3,2,1:T(8,128)} %fusion.19, f32[512,1,8,512]{0,3,2,1:T(8,128)} %fusion.22), kind=kLoop, calls=%fused_computation.24 | loop fusion | flops 4194304 | bytes 33554432 | tf_op jit(solution)/shard_map/stack | solution.py:35
  142.2 0.0 reduce-scatter.2.cloned.1.call-update
  142.2 0.2 all-gather.3.cloned.1.call-start
  142.5 282.9 %reduce-scatter.2.cloned.1.call-done = f32[512,2,8,128]{0,3,2,1:T(8,128)} async-done(((f32[512,2,8,512]{0,3,2,1:T(8,128)}), f32[512,2,8,128]{0,3,2,1:T(8,128)}) %reduce-scatter.2.cloned.1.call-update) | async-done | bytes 4194320 | tf_op jit(solution)/shard_map/reduce_scatter | solution.py:36
  425.4 2.5 convert_element_type.19
  427.9 3.1 copy.9
  430.9 52.7 %all_to_all.18 = bf16[512,2,8,128]{3,2,1,0:T(8,128)(2,1)S(1)} all-to-all(bf16[512,2,8,128]{3,2,1,0:T(8,128)(2,1)} %copy.9), channel_id=1, replica_groups=mesh['node'=4,'drow'=4,'dcol'=2] {'node'}, dimensions={0} | all-to-all | bytes 4194304 | tf_op jit(solution)/shard_map/all_to_all | solution.py:39
  483.6 1.6 copy.14
  485.2 2.3 all_to_all.16
  487.5 0.0 all-gather.3.cloned.1.call-update
  487.5 0.0 all-gather.5.cloned.1.call-start
  487.6 2.2 broadcast_in_dim.4
  489.8 0.0 all-gather.5.cloned.1.call-update
  489.8 53.8 %all-gather.3.cloned.1.call-done = bf16[256,2,8,512]{3,0,2,1:T(8,128)(2,1)} async-done(((bf16[128,2,8,512]{3,0,2,1:T(8,128)(2,1)}), bf16[256,2,8,512]{3,0,2,1:T(8,128)(2,1)}) %all-gather.3.cloned.1.call-update) | async-done | bytes 4194320 | tf_op jit(solution)/shard_map/all_gather | solution.py:42
  543.6 1.7 fusion.30
  545.4 4.6 slice_bitcast_fusion.5
  549.9 163.4 %all-gather.5.cloned.1.call-done = bf16[16,128,2,8,512]{4,1,0,3,2:T(8,128)(2,1)} async-done(((bf16[1,128,2,8,512]{4,1,0,3,2:T(8,128)(2,1)}), bf16[16,128,2,8,512]{4,1,0,3,2:T(8,128)(2,1)}) %all-gather.5.cloned.1.call-update) | async-done | bytes 33554448 | tf_op jit(solution)/shard_map/all_gather | solution.py:40
  713.4 23.0 %slice_bitcast_fusion.1 = (bf16[16,128,8,512]{3,1,0,2:T(8,128)(2,1)}, bf16[16,128,8,512]{3,1,0,2:T(8,128)(2,1)}) fusion(bf16[16,128,2,8,512]{4,1,0,3,2:T(8,128)(2,1)} %all-gather.5.cloned.1.call-done), kind=kLoop, calls=%fused_computation.15 | loop fusion | bytes 67108864 | tf_op jit(solution)/shard_map/squeeze | solution.py:41
  736.3 22.8 %pad_maximum_fusion = bf16[16,128,8,1024]{3,1,0,2:T(8,128)(2,1)} fusion(bf16[16,128,8,512]{3,1,0,2:T(8,128)(2,1)} %get-tuple-element.6, bf16[16,128,8,512]{3,1,0,2:T(8,128)(2,1)} %get-tuple-element.5), kind=kLoop, calls=%fused_computation | loop fusion | flops 67108864 | bytes 67108864 | tf_op jit(solution)/shard_map/concatenate | solution.py:41
  759.1 20.3 %convolution_bitcast_fusion.1 = f32[1,8,256,2048]{3,2,1,0:T(8,128)} fusion(bf16[8,1024,2048]{1,2,0:T(8,128)(2,1)} %bitcast.55, bf16[256,8,512]{2,0,1:T(8,128)(2,1)} %get-tuple-element.10, bf16[256,8,512]{2,0,1:T(8,128)(2,1)} %get-tuple-element.9), kind=kOutput, calls=%fused_computation.30 | convolution fusion | flops 8598323200 | bytes 54525952
  779.4 19.6 %convolution_bitcast_fusion = f32[1,8,256,2048]{3,2,1,0:T(8,128)} fusion(bf16[8,1024,2048]{1,2,0:T(8,128)(2,1)} %bitcast.56, bf16[256,8,512]{2,0,1:T(8,128)(2,1)S(1)} %fusion.30, bf16[256,8,512]{2,0,1:T(8,128)(2,1)} %get-tuple-element.10), kind=kOutput, calls=%fused_computation.29 | convolution fusion | flops 8598323200 | bytes 54525952
  799.1 23.3 %maximum_bitcast_fusion = f32[2,8,1,256,2048]{4,3,2,1,0:T(8,128)} fusion(f32[1,8,256,2048]{3,2,1,0:T(8,128)} %convolution_bitcast_fusion, f32[1,8,256,2048]{3,2,1,0:T(8,128)} %convolution_bitcast_fusion.1), kind=kLoop, calls=%fused_computation.1 | loop fusion | flops 8388608 | bytes 67108864 | tf_op jit(solution)/shard_map/broadcast_in_dim | solution.py:50
  (5 shorter events, 0.0 us)
Async XLA Ops:
  6.5 418.9 %reduce-scatter.2.cloned.1.call-start = ((), (), s32[]{:S(2)}) async-start(), calls=%async_computation.2 | async-start | bytes 20971520 | tf_op jit(solution)/shard_map/reduce_scatter | solution.py:36
  6.5 19.0 %copy-start.1 = (s32[2,1024]{1,0:T(2,128)S(1)}, s32[2,1024]{1,0:T(2,128)}, u32[]{:S(2)}) copy-start(s32[2,1024]{1,0:T(2,128)} %param.5) | copy-start | bytes 24580
  18.3 7.2 copy-start.2
  18.3 7.2 copy-start
  25.9 88.3 %slice-start = ((s8[8388608]{0:T(1024)(128)(4,1)}), s8[4194304]{0:T(1024)(128)(4,1)S(1)}, s32[]{:S(2)}) async-start(s8[8388608]{0:T(1024)(128)(4,1)} %bitcast.59), calls=%async_computation.5 | async-start | bytes 8388608
  97.0 17.3 %slice-start.1 = ((s8[8388608]{0:T(1024)(128)(4,1)}), s8[4194304]{0:T(1024)(128)(4,1)S(1)}, s32[]{:S(2)}) async-start(s8[8388608]{0:T(1024)(128)(4,1)} %bitcast.59), calls=%async_computation.6 | async-start | bytes 8388608
  142.2 401.4 %all-gather.3.cloned.1.call-start = ((), (), s32[]{:S(2)}) async-start(), calls=%async_computation.3 | async-start | bytes 6291456 | tf_op jit(solution)/shard_map/all_gather | solution.py:42
  487.5 225.8 %all-gather.5.cloned.1.call-start = ((), (), s32[]{:S(2)}) async-start(), calls=%async_computation.4 | async-start | bytes 35651584 | tf_op jit(solution)/shard_map/all_gather | solution.py:40
Sparse Core Ops, SparseCore 0:
  142.4 283.0 reduce-scatter.1
  487.6 55.9 all-gather.2
  545.3 168.0 all-gather.4
where the time goes:
time: 829 us
  waiting for transfers between devices  500 us (60%)
  other arithmetic  141 us (17%)
  matrix products  73.4 us (9%)
  blocking collectives  52.7 us (6%)
  local copies, waits for them, and re-layouts  48.5 us (6%)
  between operations  13.2 us (2%)
    reduce_scatter x1, waiting for transfers between devices, local(): lax.psum_scatter(partial_amp, 'node', scatter_dimension=3, tiled=True)  283 us
    all_gather x1, waiting for transfers between devices, local(): lax.all_gather(amplitudes[None], ('node', 'drow'), axis=0, tiled=True)  163 us
    convert_element_type x1, other arithmetic, excitation(): load_im = (-spread * jnp.sin(phase_angle)).astype(jnp.bfloat16)  71.1 us
    all_gather x1, waiting for transfers between devices, local(): row_piece = lax.all_gather(amplitudes, 'dcol', axis=0, tiled=True)  53.8 us
    all_to_all x1, blocking collectives, local(): lax.all_to_all(by_dirs, 'node', split_axis=0, concat_axis=3, tiled=True)  52.7 us
    unnamed x2, matrix products  39.9 us
    broadcast_in_dim x1, other arithmetic, local(): return jnp.stack([spec_re, spec_im], axis=0)[:, :, None]  23.3 us
    squeeze x1, local copies, waits for them, and re-layouts, local(): col_cat = jnp.concatenate([colset[:, :, 0], colset[:, :, 1]], axis=-1)  23 us
  transfers between devices with their start and end apart: 3, of which 3 were waited for; matrix products, arithmetic and copies ran while one was open for 1% of the time, Pallas kernels for 0%

commit v1 on v0

v1 whole, which is shorter than its diff:
```python
import functools
import math

import jax
import jax.numpy as jnp
from jax import lax
from jax.experimental import pallas as pl
from jax.experimental.pallas import tpu as pltpu
from jax.sharding import PartitionSpec as P

GRID = 1024
MIB = 1024 * 1024
MESH = pl.DeviceIdType.MESH


def unit_phase(turn):
    quarter = (turn + GRID // 8) >> 8
    rest = (turn - quarter * (GRID // 4)).astype(jnp.float32)
    x = rest * (2.0 * math.pi / GRID)
    x2 = x * x
    s = x * (1.0 + x2 * (-1.0 / 6 + x2 * (1.0 / 120 + x2 * (-1.0 / 5040 + x2 * (1.0 / 362880)))))
    c = 1.0 + x2 * (-0.5 + x2 * (1.0 / 24 + x2 * (-1.0 / 720 + x2 * (1.0 / 40320))))
    odd = (quarter & 1) == 1
    cos = jnp.where(odd, s, c)
    sin = jnp.where(odd, c, s)
    q = quarter & 3
    cos = jnp.where((q == 1) | (q == 2), -cos, cos)
    sin = jnp.where(q >= 2, -sin, sin)
    return cos, sin


def amp_kernel(coords_ref, steps_ref, weight_ref, h_ref, out_ref, c1, s1, cf, sf):
    nodes, dirs = c1.shape
    f = pl.program_id(0)

    @pl.when(f == 0)
    def _():
        project = (
            coords_ref[:, 0:1] * steps_ref[0:1, :] + coords_ref[:, 1:2] * steps_ref[1:2, :]
        )
        cos, sin = unit_phase(project & (GRID - 1))
        c1[...] = cos
        s1[...] = sin
        cf[...] = cos
        sf[...] = sin

    @pl.when(f > 0)
    def _():
        c, s = cf[...], sf[...]
        cf[...] = c * c1[...] - s * s1[...]
        sf[...] = s * c1[...] + c * s1[...]

    w = weight_ref[0]
    load_re = (w * cf[...]).astype(jnp.bfloat16)
    load_im = (-w * sf[...]).astype(jnp.bfloat16)
    h_re, h_im = h_ref[0, 0], h_ref[1, 0]
    dot = functools.partial(jnp.dot, preferred_element_type=jnp.float32)
    out_ref[0, :, :dirs] = (dot(h_re, load_re) - dot(h_im, load_im)).astype(jnp.bfloat16)
    out_ref[0, :, dirs:] = (dot(h_re, load_im) + dot(h_im, load_re)).astype(jnp.bfloat16)


def share_kernel(
    n_node, n_dcol, part, col_ref, row_ref, up, down, piece,
    up_s, up_r, dn_s, dn_r, zu_s, zd_s, z_r, x_s, x_r, c_s, c_r, y_s, y_r, loc,
):
    freqs = part.shape[0]
    n = lax.axis_index("node")
    r = lax.axis_index("drow")
    c = lax.axis_index("dcol")
    rx = (r + 2) % 4
    rc = r + 1 - 2 * (r % 2)
    far = rc + 2 - 4 * (rc // 2)
    above, below = {"node": n + 1}, {"node": n - 1}
    has_up, has_dn = n < n_node - 1, n > 0

    def remote(src, dst, send, recv, where):
        return pltpu.make_async_remote_copy(
            src_ref=src, dst_ref=dst, send_sem=send, recv_sem=recv,
            device_id=where, device_id_type=MESH,
        )

    def other(k):
        return (c + k) % n_dcol

    barrier = pltpu.get_barrier_semaphore()

    def greet(where):
        pl.semaphore_signal(barrier, inc=1, device_id=where, device_id_type=MESH)

    pl.when(has_up)(lambda: greet(above))
    pl.when(has_dn)(lambda: greet(below))
    greet({"drow": rx})
    greet({"drow": rc})
    for k in range(1, n_dcol):
        greet({"dcol": other(k)})
    peers = 1 + n_dcol + has_up.astype(jnp.int32) + has_dn.astype(jnp.int32)
    pl.semaphore_wait(barrier, peers)

    def hop_up(f, t, src):
        return remote(src.at[f, t], up.at[f, t], up_s.at[f, t], up_r.at[f, t], above)

    def hop_dn(f, t, src):
        return remote(src.at[f, t], down.at[f, t], dn_s.at[f, t], dn_r.at[f, t], below)

    def add(buf, f, t):
        buf[f, t] = (
            buf[f, t].astype(jnp.float32) + part[f, t].astype(jnp.float32)
        ).astype(jnp.bfloat16)

    def z_up(f, s, src):
        return remote(src, col_ref.at[f, s, r], zu_s.at[f, s], z_r.at[f, s], above)

    def z_dn(f, s, src):
        return remote(src, col_ref.at[f, s, r], zd_s.at[f, s], z_r.at[f, s], below)

    def to_x(f, s, src):
        return remote(src, col_ref.at[f, s, r], x_s.at[f, s], x_r.at[f, s], {"drow": rx})

    def to_core(f, s, q, src):
        row = r if q == 0 else rx
        return remote(
            src, col_ref.at[f, s, row], c_s.at[f, q, s], c_r.at[f, q, s], {"drow": rc}
        )

    def to_y(f, k):
        return remote(
            piece.at[f], row_ref.at[f, c], y_s.at[f, k], y_r.at[f, k], {"dcol": other(k)}
        )

    def own_col(f):
        return pltpu.make_async_copy(piece.at[f], col_ref.at[f, n, r], loc.at[f, 0])

    def own_row(f):
        return pltpu.make_async_copy(piece.at[f], row_ref.at[f, c], loc.at[f, 1])

    def hops(f):
        for k in range(n_node - 1):
            t = n_node - 1 - k

            @pl.when((t > n) & (n == 0))
            def _():
                hop_up(f, t, part).start()

            @pl.when((t > n) & (n > 0))
            def _():
                hop_up(f, t, up).wait_recv()
                add(up, f, t)
                hop_up(f, t, up).start()

            t2 = k

            @pl.when((t2 < n) & (n == n_node - 1))
            def _():
                hop_dn(f, t2, part).start()

            @pl.when((t2 < n) & (n < n_node - 1))
            def _():
                hop_dn(f, t2, down).wait_recv()
                add(down, f, t2)
                hop_dn(f, t2, down).start()

    def finish(f):
        @pl.when(has_dn)
        def _():
            hop_up(f, n, up).wait_recv()

        @pl.when(has_up)
        def _():
            hop_dn(f, n, down).wait_recv()

        own = part[f, n].astype(jnp.float32)

        @pl.when(n == 0)
        def _():
            piece[f] = (own + down[f, n].astype(jnp.float32)).astype(jnp.bfloat16)

        @pl.when(n == n_node - 1)
        def _():
            piece[f] = (own + up[f, n].astype(jnp.float32)).astype(jnp.bfloat16)

        @pl.when(has_up & has_dn)
        def _():
            piece[f] = (
                own + up[f, n].astype(jnp.float32) + down[f, n].astype(jnp.float32)
            ).astype(jnp.bfloat16)

        src = piece.at[f]
        pl.when(has_up)(lambda: z_up(f, n, src).start())
        pl.when(has_dn)(lambda: z_dn(f, n, src).start())
        to_x(f, n, src).start()
        to_core(f, n, 0, src).start()
        for k in range(1, n_dcol):
            to_y(f, k).start()
        own_col(f).start()
        own_row(f).start()

    def spread(f):
        for d in range(1, n_node):
            lo, hi = n - d, n + d

            @pl.when(lo >= 0)
            def _():
                src = col_ref.at[f, lo, r]
                z_up(f, lo, src).wait_recv()
                pl.when(has_up)(lambda: z_up(f, lo, src).start())
                to_x(f, lo, src).start()
                to_core(f, lo, 0, src).start()

            @pl.when(hi < n_node)
            def _():
                src = col_ref.at[f, hi, r]
                z_dn(f, hi, src).wait_recv()
                pl.when(has_dn)(lambda: z_dn(f, hi, src).start())
                to_x(f, hi, src).start()
                to_core(f, hi, 0, src).start()

    def crossed(f):
        for s in range(n_node):
            src = col_ref.at[f, s, rx]
            remote(src, src, x_s.at[f, s], x_r.at[f, s], {"drow": rx}).wait_recv()
            to_core(f, s, 1, src).start()

    def settle(f):
        src = piece.at[f]
        own_col(f).wait()
        own_row(f).wait()
        for k in range(1, n_dcol):
            to_y(f, k).wait_send()
            to_y(f, k).wait_recv()
        for s in range(n_node):
            to_x(f, s, src).wait_send()
            for q in range(2):
                dst = col_ref.at[f, s, rc if q == 0 else far]
                to_core(f, s, q, src).wait_send()
                remote(
                    dst, dst, c_s.at[f, q, s], c_r.at[f, q, s], {"drow": rc}
                ).wait_recv()

            pl.when(has_up & (n >= s))(lambda: z_up(f, s, src).wait_send())
            pl.when(has_dn & (n <= s))(lambda: z_dn(f, s, src).wait_send())
            pl.when(s > n)(lambda: hop_up(f, s, part).wait_send())
            pl.when(s < n)(lambda: hop_dn(f, s, part).wait_send())

    @pl.loop(0, freqs + 3)
    def _(i):
        pl.when(i < freqs)(lambda: hops(i))
        pl.when((i >= 1) & (i < freqs + 1))(lambda: finish(i - 1))
        pl.when((i >= 2) & (i < freqs + 2))(lambda: spread(i - 2))
        pl.when(i >= 3)(lambda: crossed(i - 3))

    @pl.loop(0, freqs)
    def _(f):
        settle(f)


def spec_kernel(row_ref, col_ref, out_ref):
    row = row_ref[0]
    half = row.shape[1] // 2
    turned = jnp.concatenate([row[:, half:], -row[:, :half]], axis=1)
    col = col_ref[0]
    dims = (((1,), (1,)), ((), ()))
    out_ref[0, 0, 0] = lax.dot_general(row, col, dims, preferred_element_type=jnp.float32)
    out_ref[1, 0, 0] = lax.dot_general(turned, col, dims, preferred_element_type=jnp.float32)


def local(n_node, n_drow, n_dcol, freq_resp, node_coords, heading_steps, spectral_weights):
    _, freqs, dofs, nodes = freq_resp.shape
    dirs = heading_steps.shape[1]
    width = 2 * dirs
    rows = dofs // n_node
    weight = jnp.sqrt(spectral_weights.astype(jnp.float32) / (64.0 * 512))[:, None, :]
    part = pl.pallas_call(
        amp_kernel,
        out_shape=jax.ShapeDtypeStruct((freqs, dofs, width), jnp.bfloat16),
        grid=(freqs,),
        in_specs=[
            pl.BlockSpec((nodes, 2), lambda f: (0, 0)),
            pl.BlockSpec((2, dirs), lambda f: (0, 0)),
            pl.BlockSpec((1, 1, dirs), lambda f: (f, 0, 0)),
            pl.BlockSpec((2, 1, dofs, nodes), lambda f: (0, f, 0, 0)),
        ],
        out_specs=pl.BlockSpec((1, dofs, width), lambda f: (f, 0, 0)),
        scratch_shapes=[pltpu.VMEM((nodes, dirs), jnp.float32)] * 4,
        compiler_params=pltpu.CompilerParams(vmem_limit_bytes=48 * MIB),
    )(node_coords.T, heading_steps, weight, freq_resp)
    part = part.reshape(freqs, n_node, rows, width)

    dma = pltpu.SemaphoreType.DMA
    fn = (freqs, n_node)
    col, row = pl.pallas_call(
        functools.partial(share_kernel, n_node, n_dcol),
        out_shape=(
            jax.ShapeDtypeStruct((freqs, n_node, n_drow, rows, width), jnp.bfloat16),
            jax.ShapeDtypeStruct((freqs, n_dcol, rows, width), jnp.bfloat16),
        ),
        in_specs=[pl.BlockSpec(memory_space=pltpu.VMEM)],
        out_specs=[pl.BlockSpec(memory_space=pl.ANY)] * 2,
        scratch_shapes=[
            pltpu.VMEM((freqs, n_node, rows, width), jnp.bfloat16),
            pltpu.VMEM((freqs, n_node, rows, width), jnp.bfloat16),
            pltpu.VMEM((freqs, rows, width), jnp.bfloat16),
            dma(fn), dma(fn), dma(fn), dma(fn),
            dma(fn), dma(fn), dma(fn),
            dma(fn), dma(fn),
            dma((freqs, 2, n_node)), dma((freqs, 2, n_node)),
            dma((freqs, n_dcol)), dma((freqs, n_dcol)),
            dma((freqs, 2)),
        ],
        compiler_params=pltpu.CompilerParams(
            collective_id=0, has_side_effects=True, vmem_limit_bytes=48 * MIB
        ),
    )(part)
    col = col.reshape(freqs, n_node * n_drow * rows, width)
    row = row.reshape(freqs, n_dcol * rows, width)
    a, b = row.shape[1], col.shape[1]
    return pl.pallas_call(
        spec_kernel,
        out_shape=jax.ShapeDtypeStruct((2, freqs, 1, a, b), jnp.float32),
        grid=(freqs,),
        in_specs=[
            pl.BlockSpec((1, a, width), lambda f: (f, 0, 0)),
            pl.BlockSpec((1, b, width), lambda f: (f, 0, 0)),
        ],
        out_specs=pl.BlockSpec((2, 1, 1, a, b), lambda f: (0, f, 0, 0, 0)),
        compiler_params=pltpu.CompilerParams(vmem_limit_bytes=48 * MIB),
    )(row, col)


def solution(mesh):
    sizes = (mesh.shape["node"], mesh.shape["drow"], mesh.shape["dcol"])
    placed = (P(None, None, ("drow", "dcol"), "node"), P(None, "node"), P(), P())
    return jax.shard_map(
        functools.partial(local, *sizes),
        mesh=mesh,
        in_specs=placed,
        out_specs=P(None, None, "drow", "node", "dcol"),
        check_vma=False,
    )
```

time: 829 us -> 366 us (0.44)
  waiting for transfers between devices: 500 us -> 0 us
  Pallas kernels: 0 us -> 363 us
  other arithmetic: 141 us -> 0.73 us
  matrix products: 73.4 us -> 0 us
  blocking collectives: 52.7 us -> 0 us
  local copies, waits for them, and re-layouts: 48.5 us -> 1.61 us
  between operations: 13.2 us -> 0.04 us
    pallas_call x0 -> x3, Pallas kernels: none -> 363 us  [the longest x1 304 us: local(): pl.pallas_call(functools.partial(share_kernel, n_node, n_dcol), out_shape...]
    reduce_scatter x1 -> x0, waiting for transfers between devices: 283 us -> none  [local(): lax.psum_scatter(partial_amp, 'node', scatter_dimension=3, tiled=True)]
    all_gather x2 -> x0, waiting for transfers between devices: 217 us -> none  [the longest x1 163 us: local(): lax.all_gather(amplitudes[None], ('node', 'drow'), axis=0, tiled=True)]
    convert_element_type x2 -> x0, other arithmetic: 73.5 us -> none  [the longest x1 71.1 us: excitation(): load_im = (-spread * jnp.sin(phase_angle)).astype(jnp.bfloat16)]
    all_to_all x1 -> x0, blocking collectives: 52.7 us -> none  [local(): lax.all_to_all(by_dirs, 'node', split_axis=0, concat_axis=3, tiled=True)]
    unnamed x2 -> x0, matrix products: 39.9 us -> none
    squeeze x3 -> x0, local copies, waits for them, and re-layouts: 39.3 us -> none  [the longest x1 23 us: local(): col_cat = jnp.concatenate([colset[:, :, 0], colset[:, :, 1]], axis=-1)]
    dot_general x2 -> x0, matrix products: 33.4 us -> none  [the longest x1 17.3 us: local(): jnp.einsum('fkn,fnd->kfd', left_im, right_im, preferred_element_type=jnp....]
  transfers between devices with their start and end apart: 3 -> 0, of which waited for: 3 -> 0; matrix products, arithmetic and copies ran while one was open for 1% -> 0% of each run, Pallas kernels for 0% -> 0%
where the time goes in v1:
time: 366 us
  Pallas kernels  363 us (99%)
    pallas_call x1, Pallas kernels, local(): pl.pallas_call(functools.partial(share_kernel, n_node, n_dcol), out_shape...  304 us
    pallas_call x1, Pallas kernels, local(): pl.pallas_call(spec_kernel, out_shape=jax.ShapeDtypeStruct((2, freqs, 1,...  30.1 us
    pallas_call x1, Pallas kernels, local(): pl.pallas_call(amp_kernel, out_shape=jax.ShapeDtypeStruct((freqs, dofs, w...  29.8 us

profile of v1, /device:TPU:0, one launch (start us, length us, event | category | flops | bytes accessed | tf_op | source)
XLA Modules:
  0.0 365.9 jit_solution(5119126736395847802)
XLA Ops:
  0.0 0.7 multiply_sqrt_fusion
  0.8 0.9 copy.5
  1.7 0.0 copy-start
  1.7 0.7 copy-done
  2.4 29.8 %shard_map.46 = bf16[8,512,1024]{2,1,0:T(8,128)(2,1)} custom-call(s32[1024,2]{1,0:T(8,128)S(1)} %bitcast.5, s32[2,512]{1,0:T(2,128)S(1)} %copy-done, f32[8,1,512]{2,1,0:T(1,128)S(1)} %broadcast_in_dim.3.weight_ref, bf16[2,8,512,1024]{3,2,1,0:T(8,128)(2,1)} %h_ref.1), custom_call_target="tpu_custom_call" | custom-call | tf_op jit(solution)/shard_map/pallas_call | solution.py:272
  32.2 303.6 %shard_map.47 = (bf16[8,4,4,128,1024]{4,3,2,1,0:T(8,128)(2,1)}, bf16[8,2,128,1024]{3,2,1,0:T(8,128)(2,1)S(1)}) custom-call(bf16[8,4,128,1024]{3,2,1,0:T(8,128)(2,1)} %bitcast.6), custom_call_target="tpu_custom_call" | custom-call | tf_op jit(solution)/shard_map/pallas_call | solution.py:290
  335.8 30.1 %shard_map.48 = f32[2,8,1,256,2048]{4,3,2,1,0:T(8,128)} custom-call(bf16[8,256,1024]{2,1,0:T(8,128)(2,1)S(1)} %bitcast.4, bf16[8,2048,1024]{2,1,0:T(8,128)(2,1)} %bitcast.7), custom_call_target="tpu_custom_call" | custom-call | tf_op jit(solution)/shard_map/pallas_call | solution.py:316
  (1 shorter events, 0.0 us)
Async XLA Ops:
  1.7 0.7 copy-start

commit v2 on v1

--- a/solution.py
+++ b/solution.py
@@ -30,7 +30,6 @@
 
 
 def amp_kernel(coords_ref, steps_ref, weight_ref, h_ref, out_ref, c1, s1, cf, sf):
-    nodes, dirs = c1.shape
     f = pl.program_id(0)
 
     @pl.when(f == 0)
@@ -55,8 +54,8 @@
     load_im = (-w * sf[...]).astype(jnp.bfloat16)
     h_re, h_im = h_ref[0, 0], h_ref[1, 0]
     dot = functools.partial(jnp.dot, preferred_element_type=jnp.float32)
-    out_ref[0, :, :dirs] = (dot(h_re, load_re) - dot(h_im, load_im)).astype(jnp.bfloat16)
-    out_ref[0, :, dirs:] = (dot(h_re, load_im) + dot(h_im, load_re)).astype(jnp.bfloat16)
+    out_ref[0] = (dot(h_re, load_re) - dot(h_im, load_im)).astype(jnp.bfloat16)
+    out_ref[1] = (dot(h_re, load_im) + dot(h_im, load_re)).astype(jnp.bfloat16)
 
 
 def share_kernel(
@@ -254,24 +253,24 @@
 
 
 def spec_kernel(row_ref, col_ref, out_ref):
-    row = row_ref[0]
-    half = row.shape[1] // 2
-    turned = jnp.concatenate([row[:, half:], -row[:, :half]], axis=1)
-    col = col_ref[0]
     dims = (((1,), (1,)), ((), ()))
-    out_ref[0, 0, 0] = lax.dot_general(row, col, dims, preferred_element_type=jnp.float32)
-    out_ref[1, 0, 0] = lax.dot_general(turned, col, dims, preferred_element_type=jnp.float32)
+
+    def dot(p, q):
+        return lax.dot_general(row_ref[p], col_ref[q], dims, preferred_element_type=jnp.float32)
+
+    out_ref[0, 0, 0] = dot(0, 0) + dot(1, 1)
+    out_ref[1, 0, 0] = dot(1, 0) - dot(0, 1)
 
 
 def local(n_node, n_drow, n_dcol, freq_resp, node_coords, heading_steps, spectral_weights):
     _, freqs, dofs, nodes = freq_resp.shape
     dirs = heading_steps.shape[1]
-    width = 2 * dirs
+    width, chunks = dirs, 2 * freqs
     rows = dofs // n_node
     weight = jnp.sqrt(spectral_weights.astype(jnp.float32) / (64.0 * 512))[:, None, :]
     part = pl.pallas_call(
         amp_kernel,
-        out_shape=jax.ShapeDtypeStruct((freqs, dofs, width), jnp.bfloat16),
+        out_shape=jax.ShapeDtypeStruct((chunks, dofs, width), jnp.bfloat16),
         grid=(freqs,),
         in_specs=[
             pl.BlockSpec((nodes, 2), lambda f: (0, 0)),
@@ -279,47 +278,47 @@
             pl.BlockSpec((1, 1, dirs), lambda f: (f, 0, 0)),
             pl.BlockSpec((2, 1, dofs, nodes), lambda f: (0, f, 0, 0)),
         ],
-        out_specs=pl.BlockSpec((1, dofs, width), lambda f: (f, 0, 0)),
+        out_specs=pl.BlockSpec((2, dofs, width), lambda f: (f, 0, 0)),
         scratch_shapes=[pltpu.VMEM((nodes, dirs), jnp.float32)] * 4,
         compiler_params=pltpu.CompilerParams(vmem_limit_bytes=48 * MIB),
     )(node_coords.T, heading_steps, weight, freq_resp)
-    part = part.reshape(freqs, n_node, rows, width)
+    part = part.reshape(chunks, n_node, rows, width)
 
     dma = pltpu.SemaphoreType.DMA
-    fn = (freqs, n_node)
+    fn = (chunks, n_node)
     col, row = pl.pallas_call(
         functools.partial(share_kernel, n_node, n_dcol),
         out_shape=(
-            jax.ShapeDtypeStruct((freqs, n_node, n_drow, rows, width), jnp.bfloat16),
-            jax.ShapeDtypeStruct((freqs, n_dcol, rows, width), jnp.bfloat16),
+            jax.ShapeDtypeStruct((chunks, n_node, n_drow, rows, width), jnp.bfloat16),
+            jax.ShapeDtypeStruct((chunks, n_dcol, rows, width), jnp.bfloat16),
         ),
         in_specs=[pl.BlockSpec(memory_space=pltpu.VMEM)],
         out_specs=[pl.BlockSpec(memory_space=pl.ANY)] * 2,
         scratch_shapes=[
-            pltpu.VMEM((freqs, n_node, rows, width), jnp.bfloat16),
-            pltpu.VMEM((freqs, n_node, rows, width), jnp.bfloat16),
-            pltpu.VMEM((freqs, rows, width), jnp.bfloat16),
+            pltpu.VMEM((chunks, n_node, rows, width), jnp.bfloat16),
+            pltpu.VMEM((chunks, n_node, rows, width), jnp.bfloat16),
+            pltpu.VMEM((chunks, rows, width), jnp.bfloat16),
             dma(fn), dma(fn), dma(fn), dma(fn),
             dma(fn), dma(fn), dma(fn),
             dma(fn), dma(fn),
-            dma((freqs, 2, n_node)), dma((freqs, 2, n_node)),
-            dma((freqs, n_dcol)), dma((freqs, n_dcol)),
-            dma((freqs, 2)),
+            dma((chunks, 2, n_node)), dma((chunks, 2, n_node)),
+            dma((chunks, n_dcol)), dma((chunks, n_dcol)),
+            dma((chunks, 2)),
         ],
         compiler_params=pltpu.CompilerParams(
             collective_id=0, has_side_effects=True, vmem_limit_bytes=48 * MIB
         ),
     )(part)
-    col = col.reshape(freqs, n_node * n_drow * rows, width)
-    row = row.reshape(freqs, n_dcol * rows, width)
+    col = col.reshape(chunks, n_node * n_drow * rows, width)
+    row = row.reshape(chunks, n_dcol * rows, width)
     a, b = row.shape[1], col.shape[1]
     return pl.pallas_call(
         spec_kernel,
         out_shape=jax.ShapeDtypeStruct((2, freqs, 1, a, b), jnp.float32),
         grid=(freqs,),
         in_specs=[
-            pl.BlockSpec((1, a, width), lambda f: (f, 0, 0)),
-            pl.BlockSpec((1, b, width), lambda f: (f, 0, 0)),
+            pl.BlockSpec((2, a, width), lambda f: (f, 0, 0)),
+            pl.BlockSpec((2, b, width), lambda f: (f, 0, 0)),
         ],
         out_specs=pl.BlockSpec((2, 1, 1, a, b), lambda f: (0, f, 0, 0, 0)),
         compiler_params=pltpu.CompilerParams(vmem_limit_bytes=48 * MIB),

time: 366 us -> 439 us (1.20)
  Pallas kernels: 363 us -> 436 us
    pallas_call x1, Pallas kernels: 304 us -> 376 us  [local(): pl.pallas_call(functools.partial(share_kernel, n_node, n_dcol), out_shape...]
where the time goes in v2:
time: 439 us; the launch traced here: 438 us
  Pallas kernels  436 us (99%)
    pallas_call x1, Pallas kernels, local(): pl.pallas_call(functools.partial(share_kernel, n_node, n_dcol), out_shape...  376 us
    pallas_call x1, Pallas kernels, local(): pl.pallas_call(spec_kernel, out_shape=jax.ShapeDtypeStruct((2, freqs, 1,...  30.1 us
    pallas_call x1, Pallas kernels, local(): pl.pallas_call(amp_kernel, out_shape=jax.ShapeDtypeStruct((chunks, dofs,...  29.8 us

profile of v2, /device:TPU:0, one launch (start us, length us, event | category | flops | bytes accessed | tf_op | source)
XLA Modules:
  0.0 438.4 jit_solution(15924076027637382764)
XLA Ops:
  0.0 0.7 multiply_sqrt_fusion
  0.8 0.9 copy.5
  1.7 0.0 copy-start
  1.7 0.7 copy-done
  2.4 29.8 %shard_map.46 = bf16[16,512,512]{2,1,0:T(8,128)(2,1)} custom-call(s32[1024,2]{1,0:T(8,128)S(1)} %bitcast.5, s32[2,512]{1,0:T(2,128)S(1)} %copy-done, f32[8,1,512]{2,1,0:T(1,128)S(1)} %broadcast_in_dim.3.weight_ref, bf16[2,8,512,1024]{3,2,1,0:T(8,128)(2,1)} %h_ref.1), custom_call_target="tpu_custom_call" | custom-call | tf_op jit(solution)/shard_map/pallas_call | solution.py:271
  32.2 376.1 %shard_map.47 = (bf16[16,4,4,128,512]{4,3,2,1,0:T(8,128)(2,1)}, bf16[16,2,128,512]{3,2,1,0:T(8,128)(2,1)S(1)}) custom-call(bf16[16,4,128,512]{3,2,1,0:T(8,128)(2,1)} %bitcast.6), custom_call_target="tpu_custom_call" | custom-call | tf_op jit(solution)/shard_map/pallas_call | solution.py:289
  408.3 30.1 %shard_map.48 = f32[2,8,1,256,2048]{4,3,2,1,0:T(8,128)} custom-call(bf16[16,256,512]{2,1,0:T(8,128)(2,1)S(1)} %bitcast.4, bf16[16,2048,512]{2,1,0:T(8,128)(2,1)} %bitcast.7), custom_call_target="tpu_custom_call" | custom-call | tf_op jit(solution)/shard_map/pallas_call | solution.py:315
  (1 shorter events, 0.0 us)
Async XLA Ops:
  1.7 0.7 copy-start
